TPU v7x, 32 devices: a whole 2x2x4 slice. The times are simulated.
32 devices in a mesh: dp: 4 (over z), row: 2 (over core), col: 4 (over y, x).
Axes of the slice: x: 2, y: 2, z: 4, core: 2. Of those that a mesh axis runs over, the one named last changes fastest.
Arguments:
- features: bfloat16 [2048, 4096], P(('dp', 'row')), may hold values from -6 to 6
- w_in: bfloat16 [4096, 4096], P('row', 'col'), may hold values from -0.09375 to 0.09375
- w_out: bfloat16 [4096, 1024], P('col'), may hold values from -0.09375 to 0.09375
- captions: bfloat16 [2048, 1024], P(('dp', 'row', 'col')), may hold values from -6 to 6
- positive: int32 [2048], P(('dp', 'row')), may hold values from 0 to 2047, each once
Outputs:
- fig_terms: float32 [2048], P(('dp', 'row'))
- cap_terms: float32 [2048], P(('dp', 'row', 'col'))
- grad_w_in: float32 [4096, 4096], P(('dp', 'row'), 'col')
- grad_w_out: float32 [4096, 1024], P('col', ('dp', 'row'))
Inputs may be any that keep to these rules, and one draw needn't show every extreme that they name: positive is a permutation: every caption is the match of exactly one figure.
All inputs are finite; a program needn't handle non-finite values.
Results may differ from a plain program's by a relative error of at most 0.0053.
Values may be sent and summed in bfloat16 or wider, within the bound.
A program may use at most 128 MiB of HBM per device.

v0:
```python
import jax
import jax.numpy as jnp
from jax import lax
from jax.sharding import PartitionSpec as P

SCALE = 50.0
EPS = 1e-06


def gelu_back(pre, grad):
    return jax.vjp(jax.nn.gelu, pre)[1](grad)[0]


def on_device(features, w_in, w_out, captions, positive):
    columns = features
    pre = jnp.dot(
        columns, lax.all_gather(w_in, "row", axis=0, tiled=True), preferred_element_type=jnp.float32
    )
    hidden = jax.nn.gelu(pre).astype(jnp.bfloat16)
    emb = lax.psum(jnp.dot(hidden, w_out, preferred_element_type=jnp.float32), "col")
    inv = lax.rsqrt(jnp.sum(emb * emb, axis=1, keepdims=True) + EPS)
    fhat = emb * inv
    fhat_b = fhat.astype(jnp.bfloat16)
    cap32 = captions.astype(jnp.float32)
    chat_local = (cap32 * lax.rsqrt(jnp.sum(cap32 * cap32, axis=1, keepdims=True) + EPS)).astype(
        jnp.bfloat16
    )
    block = lax.all_gather(chat_local, ("dp", "row"), axis=0, tiled=True)
    capdev = captions.shape[0]
    ncol = lax.axis_size("col")
    places = jnp.arange(block.shape[0], dtype=jnp.int32)
    colids = (places // capdev * ncol + lax.axis_index("col")) * capdev + places % capdev
    logits = SCALE * lax.dot_general(
        fhat_b, block, (((1,), (1,)), ((), ())), preferred_element_type=jnp.float32
    )
    mask = (positive[:, None] == colids[None, :]).astype(jnp.float32)
    expo = jnp.exp(logits)
    picked = mask * logits
    rowsum, rowpos = lax.psum((jnp.sum(expo, axis=1), jnp.sum(picked, axis=1)), "col")
    colsum, colpos = lax.psum((jnp.sum(expo, axis=0), jnp.sum(picked, axis=0)), ("dp", "row"))
    fig_terms = jnp.log(rowsum) - rowpos
    group = lax.axis_index("dp") * lax.axis_size("row") + lax.axis_index("row")
    cap_all = jnp.log(colsum) - colpos
    cap_terms = lax.dynamic_slice_in_dim(cap_all, group * capdev, capdev, 0)
    dlog = (expo / rowsum[:, None] + expo / colsum[None, :] - 2.0 * mask).astype(jnp.bfloat16)
    direction = SCALE * jnp.dot(dlog, block, preferred_element_type=jnp.float32)
    dfhat = lax.psum(direction, "col")
    demb = ((dfhat - fhat * jnp.sum(fhat * dfhat, axis=1, keepdims=True)) * inv).astype(
        jnp.bfloat16
    )
    dh = lax.dot_general(demb, w_out, (((1,), (1,)), ((), ())), preferred_element_type=jnp.float32)
    dpre = gelu_back(pre, dh).astype(jnp.bfloat16)
    head_term = lax.dot_general(
        hidden, demb, (((0,), (0,)), ((), ())), preferred_element_type=jnp.float32
    )
    grad_w_out = lax.psum_scatter(head_term, ("dp", "row"), scatter_dimension=1, tiled=True)
    columns = features
    grad_w_in = lax.psum_scatter(
        lax.dot_general(
            columns, dpre, (((0,), (0,)), ((), ())), preferred_element_type=jnp.float32
        ),
        ("dp", "row"),
        scatter_dimension=0,
        tiled=True,
    )
    return (fig_terms, cap_terms, grad_w_in, grad_w_out)


def solution(mesh):
    placed = (
        P(("dp", "row"), None),
        P("row", "col"),
        P("col", None),
        P(("dp", "row", "col"), None),
        P(("dp", "row")),
    )
    return jax.shard_map(
        on_device,
        mesh=mesh,
        in_specs=placed,
        out_specs=(
            P(("dp", "row")),
            P(("dp", "row", "col")),
            P(("dp", "row"), "col"),
            P("col", ("dp", "row")),
        ),
        check_vma=False,
    )
```

profile of v0, /device:TPU:0, one launch (start us, length us, event | category | flops | bytes accessed | tf_op | source)
XLA Modules:
  0.0 419.0 jit_solution(432756732322447782)
XLA Ops:
  8.0 0.0 copy-start
  8.0 0.0 all-gather.3.cloned.1.call-start
  8.1 0.7 all-gather.3.cloned.1.call-update
  8.7 0.0 all-reduce.5.cloned.1.call-start
  8.8 24.2 %all-gather.3.cloned.1.call-done = bf16[4096,1024]{1,0:T(8,128)(2,1)} async-done(((bf16[2048,1024]{1,0:T(8,128)(2,1)}), bf16[4096,1024]{1,0:T(8,128)(2,1)}) %all-gather.3.cloned.1.call-update) | async-done | bytes 8388624 | tf_op jit(solution)/shard_map/all_gather | solution.py:17
  33.0 6.3 %fusion.51 = f32[256,1024]{1,0:T(8,128)S(1)} fusion(bf16[256,4096]{1,0:T(8,128)(2,1)} %param.5, bf16[4096,1024]{1,0:T(8,128)(2,1)} %all-gather.3.cloned.1.call-done), kind=kOutput, calls=%fused_computation.72 | convolution fusion | flops 2147483648 | bytes 11534336 | tf_op jit(solution)/shard_map/dot_general | solution.py:16
  39.3 0.0 copy-start.4
  39.3 1.0 copy-done.4
  40.3 0.0 copy-done
  40.3 0.0 copy-start.5
  40.3 1.8 fusion.48
  42.1 0.0 copy-start.6
  42.1 0.0 all-reduce.5.cloned.1.call-update
  42.2 0.0 all-gather.5.cloned.1.call-start
  42.2 0.0 copy-done.5
  42.2 0.1 fusion.20
  42.4 0.8 fusion.21
  43.1 0.0 all-gather.5.cloned.1.call-update
  43.1 0.0 all-reduce.7.cloned.1.call-start
  43.2 52.8 %all-reduce.5.cloned.1.call-done = f32[256,1024]{1,0:T(8,128)} async-done(((f32[256,1024]{1,0:T(8,128)}), f32[256,1024]{1,0:T(8,128)}) %all-reduce.5.cloned.1.call-update) | async-done | bytes 1048592 | tf_op jit(solution)/shard_map/psum | solution.py:20
  96.0 1.4 multiply_reduce_fusion.1
  97.4 0.0 all-gather.5.cloned.1.call-done
  97.5 0.0 copy-done.6
  97.5 2.9 fusion.17
  100.4 16.3 %all-reduce = (f32[512]{0:T(512)S(1)}, f32[512]{0:T(512)S(1)}) all-reduce(f32[512]{0:T(512)S(1)} %get-tuple-element.8, f32[512]{0:T(512)S(1)} %get-tuple-element.10), channel_id=1, replica_groups=mesh['dp'=4,'row'=2,'col'=4] {'dp','row'}, use_global_device_ids=true, to_apply=%region_10.11 | all-reduce | flops 1024 | bytes 8192 | tf_op jit(solution)/shard_map/psum | solution.py:40
  116.7 8.9 %all-reduce.1 = (f32[256]{0:T(256)S(1)}, f32[256]{0:T(256)S(1)}) all-reduce(f32[256]{0:T(256)S(1)} %get-tuple-element.9, f32[256]{0:T(256)S(1)} %get-tuple-element.11), channel_id=1, replica_groups=mesh['dp'=4,'row'=2,'col'=4] {'col'}, use_global_device_ids=true, to_apply=%region_6.7 | all-reduce | flops 512 | bytes 4096 | tf_op jit(solution)/shard_map/psum | solution.py:39
  125.6 0.0 copy-start.1
  125.6 3.0 convolution_multiply_fusion
  128.6 0.0 all-reduce.7.cloned.1.call-update
  128.6 0.0 reduce-scatter.3.cloned.1.call-start
  128.7 49.9 %all-reduce.7.cloned.1.call-done = f32[256,1024]{1,0:T(8,128)} async-done(((f32[256,1024]{1,0:T(8,128)}), f32[256,1024]{1,0:T(8,128)}) %all-reduce.7.cloned.1.call-update) | async-done | bytes 1048592 | tf_op jit(solution)/shard_map/psum | solution.py:47
  178.6 0.0 copy-done.1
  178.6 0.0 copy-start.3
  178.6 1.6 multiply_reduce_fusion
  180.1 0.0 copy-done.3
  180.2 1.0 multiply_convert_fusion
  181.2 11.2 %convolution_bitcast_fusion = f32[4096,1024]{0,1:T(8,128)} fusion(bf16[256,4096]{1,0:T(8,128)(2,1)} %param.5, f32[256,1024]{1,0:T(8,128)} %copy-done.4, bf16[256,1024]{1,0:T(8,128)(2,1)} %multiply_convert_fusion, bf16[1024,1024]{1,0:T(8,128)(2,1)S(1)} %copy-done), kind=kOutput, calls=%fused_computation | convolution fusion | flops 2689597440 | bytes 22544384 | tf_op jit(solution)/shard_map/dot_general | solution.py:59
  192.4 0.0 copy-start.2
  192.4 0.0 reduce-scatter.3.cloned.1.call-update
  192.4 0.0 reduce-scatter.5.cloned.1.call-start
  192.5 1.0 copy-done.2
  193.5 4.0 fusion.47
  197.5 0.0 reduce-scatter.5.cloned.1.call-update
  197.5 0.6 dynamic_slice.3
  198.1 0.6 log_subtract_fusion.1
  198.7 161.9 %reduce-scatter.3.cloned.1.call-done = f32[512,1024]{0,1:T(8,128)} async-done(((f32[4096,1024]{0,1:T(8,128)}), f32[512,1024]{0,1:T(8,128)}) %reduce-scatter.3.cloned.1.call-update) | async-done | bytes 2097168 | tf_op jit(solution)/shard_map/reduce_scatter | solution.py:58
  360.6 2.9 copy.9
  363.5 48.1 %reduce-scatter.5.cloned.1.call-done = f32[1024,128]{1,0:T(8,128)} async-done(((f32[1024,1024]{1,0:T(8,128)}), f32[1024,128]{1,0:T(8,128)}) %reduce-scatter.5.cloned.1.call-update) | async-done | bytes 524304 | tf_op jit(solution)/shard_map/reduce_scatter | solution.py:56
  (4 shorter events, 0.0 us)
Async XLA Ops:
  8.0 32.3 %copy-start = (bf16[1024,1024]{1,0:T(8,128)(2,1)S(1)}, bf16[1024,1024]{1,0:T(8,128)(2,1)}, u32[]{:S(2)}) copy-start(bf16[1024,1024]{1,0:T(8,128)(2,1)} %param.7) | copy-start | bytes 6291460
  8.0 25.0 %all-gather.3.cloned.1.call-start = ((), (), s32[]{:S(2)}) async-start(), calls=%async_computation.2 | async-start | bytes 12582912 | tf_op jit(solution)/shard_map/all_gather | solution.py:17
  8.7 87.3 %all-reduce.5.cloned.1.call-start = ((), (), s32[]{:S(2)}) async-start(), calls=%async_computation.3 | async-start | bytes 2097152 | tf_op jit(solution)/shard_map/psum | solution.py:20
  39.3 1.0 copy-start.4
  40.3 1.9 copy-start.5
  42.1 55.3 %copy-start.6 = (s32[256]{0:T(256)S(1)}, s32[256]{0:T(256)}, u32[]{:S(2)}) copy-start(s32[256]{0:T(256)} %param.9) | copy-start | bytes 3076
  42.2 55.3 %all-gather.5.cloned.1.call-start = ((), (), s32[]{:S(2)}) async-start(), calls=%async_computation.4 | async-start | bytes 1179648 | tf_op jit(solution)/shard_map/all_gather | solution.py:28
  43.1 135.4 %all-reduce.7.cloned.1.call-start = ((), (), s32[]{:S(2)}) async-start(), calls=%async_computation.5 | async-start | bytes 2097152 | tf_op jit(solution)/shard_map/psum | solution.py:47
  125.6 53.0 %copy-start.1 = (f32[256,1024]{1,0:T(8,128)S(1)}, f32[256,1024]{1,0:T(8,128)}, u32[]{:S(2)}) copy-start(f32[256,1024]{1,0:T(8,128)} %all-reduce.5.cloned.1.call-done) | copy-start | bytes 3145732
  128.6 232.0 %reduce-scatter.3.cloned.1.call-start = ((), (), s32[]{:S(2)}) async-start(), calls=%async_computation.6 | async-start | bytes 18874368 | tf_op jit(solution)/shard_map/reduce_scatter | solution.py:58
  178.6 1.6 copy-start.3
  192.4 1.0 copy-start.2
  192.4 219.2 %reduce-scatter.5.cloned.1.call-start = ((), (), s32[]{:S(2)}) async-start(), calls=%async_computation.7 | async-start | bytes 4718592 | tf_op jit(solution)/shard_map/reduce_scatter | solution.py:56
Sparse Core Ops, SparseCore 0:
  10.4 22.5 all-gather.2
  42.3 53.7 all-reduce.4
  128.8 49.7 all-reduce.6
Sparse Core Ops, SparseCore 1:
  44.8 23.1 all-gather.4
  192.5 168.0 reduce-scatter.2
  363.3 48.2 reduce-scatter.4
where the time goes:
time: 419 us
  waiting for transfers between devices  338 us (81%)
  matrix products  29.3 us (7%)
  blocking collectives  25.2 us (6%)
  between operations  15.5 us (4%)
  local copies, waits for them, and re-layouts  5.45 us (1%)
  other arithmetic  5.45 us (1%)
    reduce_scatter x1, waiting for transfers between devices, on_device(): lax.psum_scatter(lax.dot_general(columns, dpre, (((0,), (0,)), ((), ())),...  162 us
    psum x1, waiting for transfers between devices, on_device(): lax.psum(jnp.dot(hidden, w_out, preferred_element_type=jnp.float32), 'col')  52.8 us
    psum x1, waiting for transfers between devices, on_device(): dfhat = lax.psum(direction, 'col')  49.9 us
    reduce_scatter x1, waiting for transfers between devices, on_device(): lax.psum_scatter(head_term, ('dp', 'row'), scatter_dimension=1, tiled=True)  48.1 us
    all_gather x1, waiting for transfers between devices, on_device(): lax.all_gather(w_in, 'row', axis=0, tiled=True)  24.2 us
    psum x1, blocking collectives, on_device(): lax.psum((jnp.sum(expo, axis=0), jnp.sum(picked, axis=0)), ('dp', 'row'))  16.3 us
    dot_general x1, matrix products, on_device(): lax.dot_general(columns, dpre, (((0,), (0,)), ((), ())), preferred_elemen...  11.2 us
    psum x1, blocking collectives, on_device(): lax.psum((jnp.sum(expo, axis=1), jnp.sum(picked, axis=1)), 'col')  8.92 us
  transfers between devices with their start and end apart: 6, of which 5 were waited for; matrix products, arithmetic and copies ran while one was open for 2% of the time, Pallas kernels for 0%

commit v1 on v0

v1 whole, which is shorter than its diff:
```python
import jax
import jax.numpy as jnp
from jax import lax
from jax.sharding import PartitionSpec as P

SCALE = 50.0
EPS = 1e-06


def gelu_back(pre, grad):
    return jax.vjp(jax.nn.gelu, pre)[1](grad)[0]


def on_device(features, w_in, w_out, captions, positive):
    group = ("dp", "row")
    every = ("dp", "row", "col")
    f32 = jnp.float32
    slices = lax.all_to_all(features, group, 1, 0, tiled=True)
    cap32 = captions.astype(f32)
    chat_local = (cap32 * lax.rsqrt(jnp.sum(cap32 * cap32, axis=1, keepdims=True) + EPS)).astype(
        jnp.bfloat16
    )
    chat = lax.all_gather(chat_local, every, axis=0, tiled=True)
    pre = jnp.dot(
        features, lax.all_gather(w_in, "row", axis=0, tiled=True), preferred_element_type=f32
    )
    hidden = jax.nn.gelu(pre).astype(jnp.bfloat16)
    part = jnp.dot(hidden, w_out, preferred_element_type=f32)
    emb = lax.psum_scatter(part, "col", scatter_dimension=0, tiled=True)
    mine = emb.shape[0]
    inv = lax.rsqrt(jnp.sum(emb * emb, axis=1, keepdims=True) + EPS)
    fhat = emb * inv
    fhat_b = fhat.astype(jnp.bfloat16)
    logits = SCALE * lax.dot_general(
        fhat_b, chat, (((1,), (1,)), ((), ())), preferred_element_type=f32
    )
    col = lax.axis_index("col")
    places = lax.dynamic_slice_in_dim(positive, col * mine, mine, 0)
    colids = jnp.arange(chat.shape[0], dtype=jnp.int32)
    mask = (places[:, None] == colids[None, :]).astype(f32)
    expo = jnp.exp(logits)
    picked = mask * logits
    rowsum, rowpos = jnp.sum(expo, axis=1), jnp.sum(picked, axis=1)
    colsum, colpos = lax.psum((jnp.sum(expo, axis=0), jnp.sum(picked, axis=0)), every)
    fig_terms = lax.all_gather(jnp.log(rowsum) - rowpos, "col", axis=0, tiled=True)
    capdev = captions.shape[0]
    place = (lax.axis_index("dp") * lax.axis_size("row") + lax.axis_index("row")) * lax.axis_size(
        "col"
    ) + col
    cap_terms = lax.dynamic_slice_in_dim(jnp.log(colsum) - colpos, place * capdev, capdev, 0)
    dlog = (expo / rowsum[:, None] + expo / colsum[None, :] - 2.0 * mask).astype(jnp.bfloat16)
    dfhat = SCALE * jnp.dot(dlog, chat, preferred_element_type=f32)
    demb = ((dfhat - fhat * jnp.sum(fhat * dfhat, axis=1, keepdims=True)) * inv).astype(
        jnp.bfloat16
    )
    demb = lax.all_gather(demb, "col", axis=0, tiled=True)
    dh = lax.dot_general(demb, w_out, (((1,), (1,)), ((), ())), preferred_element_type=f32)
    dpre = gelu_back(pre, dh).astype(jnp.bfloat16)
    dpre_all = lax.all_gather(dpre, group, axis=0, tiled=True)
    head_term = lax.dot_general(
        hidden, demb, (((0,), (0,)), ((), ())), preferred_element_type=f32
    )
    grad_w_out = lax.psum_scatter(head_term, group, scatter_dimension=1, tiled=True)
    grad_w_in = lax.dot_general(
        slices, dpre_all, (((0,), (0,)), ((), ())), preferred_element_type=f32
    )
    return (fig_terms, cap_terms, grad_w_in, grad_w_out)


def solution(mesh):
    placed = (
        P(("dp", "row"), None),
        P("row", "col"),
        P("col", None),
        P(("dp", "row", "col"), None),
        P(("dp", "row")),
    )
    return jax.shard_map(
        on_device,
        mesh=mesh,
        in_specs=placed,
        out_specs=(
            P(("dp", "row")),
            P(("dp", "row", "col")),
            P(("dp", "row"), "col"),
            P("col", ("dp", "row")),
        ),
        check_vma=False,
    )
```

time: 419 us -> 311 us (0.74)
  waiting for transfers between devices: 338 us -> 184 us
  blocking collectives: 25.2 us -> 61.4 us
  local copies, waits for them, and re-layouts: 5.45 us -> 12.8 us
  starting transfers between devices: 0.25 us -> 4.7 us
    reduce_scatter x2, waiting for transfers between devices: 210 us -> 47.8 us  [the longest x1 28.3 us: on_device(): emb = lax.psum_scatter(part, 'col', scatter_dimension=0, tiled=True)]
    psum x2 -> x0, waiting for transfers between devices: 103 us -> none  [the longest x1 52.8 us: on_device(): lax.psum(jnp.dot(hidden, w_out, preferred_element_type=jnp.float32), 'col')]
    all_to_all x0 -> x1, waiting for transfers between devices: none -> 74.7 us  [on_device(): slices = lax.all_to_all(features, group, 1, 0, tiled=True)]
    all_gather x1 -> x2, waiting for transfers between devices: 0.02 us -> 36.8 us  [the longest x1 36.8 us: on_device(): chat = lax.all_gather(chat_local, every, axis=0, tiled=True)]
    psum x2 -> x1, blocking collectives: 25.2 us -> 39.3 us  [on_device(): lax.psum((jnp.sum(expo, axis=0), jnp.sum(picked, axis=0)), every)]
    all_gather x0 -> x1, blocking collectives: none -> 11.6 us  [on_device(): demb = lax.all_gather(demb, 'col', axis=0, tiled=True)]
    unnamed x0 -> x1, blocking collectives: none -> 10.5 us
    all_to_all x0 -> x1, starting transfers between devices: none -> 4.49 us  [on_device(): slices = lax.all_to_all(features, group, 1, 0, tiled=True)]
  transfers between devices with their start and end apart: 6 -> 6, of which waited for: 5 -> 5; matrix products, arithmetic and copies ran while one was open for 2% -> 8% of each run, Pallas kernels for 0% -> 0%
where the time goes in v1:
time: 311 us; the launch traced here: 310 us
  waiting for transfers between devices  184 us (59%)
  blocking collectives  61.4 us (20%)
  matrix products  28.1 us (9%)
  between operations  16.4 us (5%)
  local copies, waits for them, and re-layouts  12.8 us (4%)
  starting transfers between devices  4.7 us (2%)
    all_to_all x1, waiting for transfers between devices, on_device(): slices = lax.all_to_all(features, group, 1, 0, tiled=True)  74.7 us
    psum x1, blocking collectives, on_device(): lax.psum((jnp.sum(expo, axis=0), jnp.sum(picked, axis=0)), every)  39.3 us
    all_gather x1, waiting for transfers between devices, on_device(): chat = lax.all_gather(chat_local, every, axis=0, tiled=True)  36.8 us
    reduce_scatter x1, waiting for transfers between devices, on_device(): emb = lax.psum_scatter(part, 'col', scatter_dimension=0, tiled=True)  28.3 us
    all_gather x1, waiting for transfers between devices, on_device(): lax.all_gather(w_in, 'row', axis=0, tiled=True)  24.2 us
    reduce_scatter x1, waiting for transfers between devices, on_device(): lax.psum_scatter(head_term, group, scatter_dimension=1, tiled=True)  19.6 us
    all_gather x1, blocking collectives, on_device(): demb = lax.all_gather(demb, 'col', axis=0, tiled=True)  11.6 us
    unnamed x1, blocking collectives  10.5 us
  transfers between devices with their start and end apart: 6, of which 5 were waited for; matrix products, arithmetic and copies ran while one was open for 8% of the time, Pallas kernels for 0%

profile of v1, /device:TPU:0, one launch (start us, length us, event | category | flops | bytes accessed | tf_op | source)
XLA Modules:
  0.0 310.4 jit_solution(15779341503108276041)
XLA Ops:
  8.0 0.0 copy-start
  8.0 0.0 all-gather.4.cloned.1.call-start
  8.1 0.7 all-gather.4.cloned.1.call-update
  8.7 0.0 reduce-scatter.3.cloned.1.call-start
  8.8 24.2 %all-gather.4.cloned.1.call-done = bf16[4096,1024]{1,0:T(8,128)(2,1)} async-done(((bf16[2048,1024]{1,0:T(8,128)(2,1)}), bf16[4096,1024]{1,0:T(8,128)(2,1)}) %all-gather.4.cloned.1.call-update) | async-done | bytes 8388624 | tf_op jit(solution)/shard_map/all_gather | solution.py:25
  33.0 6.3 %fusion.22 = f32[256,1024]{1,0:T(8,128)S(1)} fusion(bf16[256,4096]{1,0:T(8,128)(2,1)} %param.5, bf16[4096,1024]{1,0:T(8,128)(2,1)} %all-gather.4.cloned.1.call-done), kind=kOutput, calls=%fused_computation.43 | convolution fusion | flops 2147483648 | bytes 11534336 | tf_op jit(solution)/shard_map/dot_general | solution.py:24
  39.3 0.0 copy-start.2
  39.3 1.1 copy-done.2
  40.4 0.0 copy-done
  40.4 0.0 copy-start.4
  40.4 0.0 copy-start.5
  40.4 1.8 fusion.21
  42.2 0.0 reduce-scatter.3.cloned.1.call-update
  42.2 0.0 all-gather.6.cloned.1.call-start
  42.3 0.0 copy-done.4
  42.3 0.1 fusion.10
  42.4 0.8 fusion.11
  43.2 0.0 all-gather.6.cloned.1.call-update
  43.2 0.0 all-gather.8.cloned.1.call-start
  43.3 0.0 copy-done.5
  43.3 0.1 dynamic_slice.6
  43.4 28.3 %reduce-scatter.3.cloned.1.call-done = f32[64,1024]{1,0:T(8,128)} async-done(((f32[256,1024]{1,0:T(8,128)}), f32[64,1024]{1,0:T(8,128)}) %reduce-scatter.3.cloned.1.call-update) | async-done | bytes 262160 | tf_op jit(solution)/shard_map/reduce_scatter | solution.py:29
  71.6 1.1 multiply_reduce_fusion.1
  72.7 0.0 copy-start.1
  72.7 36.8 %all-gather.6.cloned.1.call-done = bf16[2048,1024]{1,0:T(8,128)(2,1)} async-done(((bf16[64,1024]{1,0:T(8,128)(2,1)}), bf16[2048,1024]{1,0:T(8,128)(2,1)}) %all-gather.6.cloned.1.call-update) | async-done | bytes 4194320 | tf_op jit(solution)/shard_map/all_gather | solution.py:23
  109.5 3.9 %fusion.8 = (f32[2048]{0:T(1024)S(1)}, f32[64]{0:T(128)S(1)}, f32[2048]{0:T(1024)S(1)}, f32[64]{0:T(128)S(1)}, f32[64,2048]{1,0:T(8,128)S(1)}) fusion(s32[64]{0:T(128)S(1)} %dynamic_slice.6, bf16[2048,1024]{1,0:T(8,128)(2,1)} %all-gather.6.cloned.1.call-done, f32[64,1024]{1,0:T(8,128)} %reduce-scatter.3.cloned.1.call-done, f32[64]{0:T(128)S(1)} %add_rsqrt_fusion.1), kind=kOutput, calls=%fused_computation.16 | convolution fusion | flops 269479808 | bytes 4998144 | tf_op jit(solution)/shard_map/dot_general | solution.py:34
  113.4 39.3 %all-reduce.1 = (f32[2048]{0:T(1024)S(1)}, f32[2048]{0:T(1024)S(1)}) all-reduce(f32[2048]{0:T(1024)S(1)} %get-tuple-element.16, f32[2048]{0:T(1024)S(1)} %get-tuple-element.18), channel_id=1, replica_groups=mesh['dp'=4,'row'=2,'col'=4] {'dp','row','col'}, use_global_device_ids=true, to_apply=%region_8.0 | all-reduce | flops 4096 | bytes 32768 | tf_op jit(solution)/shard_map/psum | solution.py:44
  152.7 0.0 copy-done.1
  152.7 0.0 copy-start.3
  152.7 3.3 %multiply_reduce_fusion = (f32[64]{0:T(128)S(1)}, f32[64,1024]{1,0:T(8,128)S(1)}) fusion(f32[64,1024]{1,0:T(8,128)S(1)} %copy-done.1, f32[64]{0:T(128)S(1)} %add_rsqrt_fusion.1, bf16[2048,1024]{1,0:T(8,128)(2,1)} %all-gather.6.cloned.1.call-done, f32[64,2048]{1,0:T(8,128)S(1)} %get-tuple-element.22, f32[2048]{0:T(1024)S(1)} %get-tuple-element.21, ...), kind=kOutput, calls=%fused_computation.25 | convolution fusion | flops 269615040 | bytes 5252096 | tf_op jit(solution)/shard_map/dot_general | solution.py:52
  156.0 0.1 multiply_convert_fusion.1
  156.1 11.6 %all_gather.18 = bf16[256,1024]{1,0:T(8,128)(2,1)S(1)} all-gather(bf16[64,1024]{1,0:T(8,128)(2,1)S(1)} %multiply_convert_fusion.1), channel_id=1, replica_groups=mesh['dp'=4,'row'=2,'col'=4] {'col'}, dimensions={0}, use_global_device_ids=true | all-gather | bytes 655360 | tf_op jit(solution)/shard_map/all_gather | solution.py:56
  167.7 0.0 copy-done.3
  167.7 2.1 fusion.6
  169.8 0.0 all-gather.8.cloned.1.call-update
  169.8 0.0 reduce-scatter.5.cloned.1.call-start
  169.9 4.0 %fusion.20 = f32[1024,1024]{1,0:T(8,128)} fusion(bf16[256,1024]{1,0:T(8,128)(2,1)S(1)} %all_gather.18, f32[256,1024]{1,0:T(8,128)} %copy-done.2), kind=kOutput, calls=%fused_computation.41 | convolution fusion | flops 539230208 | bytes 5767168 | tf_op jit(solution)/shard_map/dot_general | solution.py:60
  173.9 0.0 reduce-scatter.5.cloned.1.call-update
  173.9 4.1 %copy.11 = bf16[256,4096]{0,1:T(8,128)(2,1)} copy(bf16[256,4096]{1,0:T(8,128)(2,1)} %param.5) | data formatting | bytes 4194304 | tf_op args[0]
  178.1 0.0 copy-start.6
  178.1 4.5 %all-to-all-start = ((bf16[256,8,512]{0,2,1:T(8,128)(2,1)}), bf16[256,8,512]{0,2,1:T(8,128)(2,1)}, u32[]{:S(2)}, u32[]{:S(2)}) async-start(bf16[256,8,512]{0,2,1:T(8,128)(2,1)} %bitcast.16), calls=%async_computation.1 | async-start | bytes 4194304 | tf_op jit(solution)/shard_map/all_to_all | solution.py:18
  182.6 0.0 copy-done.6
  182.6 0.6 dynamic-slice
  183.8 74.7 %all-to-all-done = bf16[256,8,512]{0,2,1:T(8,128)(2,1)} async-done(((bf16[256,8,512]{0,2,1:T(8,128)(2,1)}), bf16[256,8,512]{0,2,1:T(8,128)(2,1)}, u32[]{:S(2)}, u32[]{:S(2)}) %all-to-all-start) | async-done | bytes 2097184 | tf_op jit(solution)/shard_map/all_to_all | solution.py:18
  258.5 4.0 %copy.12 = bf16[8,256,512]{2,1,0:T(8,128)(2,1)} copy(bf16[8,256,512]{1,2,0:T(8,128)(2,1)} %bitcast.2) | data formatting | bytes 4194304 | tf_op jit(solution)/shard_map/all_to_all | solution.py:18
  262.5 0.1 subtract_dynamic-update-slice_fusion
  262.6 10.5 %all-reduce = f32[256]{0:T(256)} all-reduce(f32[256]{0:T(256)S(1)} %subtract_dynamic-update-slice_fusion), channel_id=1, replica_groups=mesh['dp'=4,'row'=2,'col'=4] {'col'}, use_global_device_ids=true, to_apply=%add | all-reduce | flops 256 | bytes 2048
  273.1 0.6 dynamic-slice_subtract_fusion
  273.7 0.0 all-gather.8.cloned.1.call-done
  273.7 6.7 %convolution_bitcast_fusion = f32[512,1024]{0,1:T(8,128)} fusion(bf16[2048,1024]{1,0:T(8,128)(2,1)} %all-gather.8.cloned.1.call-done, bf16[2048,512]{1,0:T(8,128)(2,1)} %bitcast.17), kind=kOutput, calls=%fused_computation.1 | convolution fusion | flops 2147483648 | bytes 8388608 | tf_op jit(solution)/shard_map/dot_general | solution.py:64
  280.4 2.9 copy.13
  283.3 19.6 %reduce-scatter.5.cloned.1.call-done = f32[1024,128]{1,0:T(8,128)} async-done(((f32[1024,1024]{1,0:T(8,128)}), f32[1024,128]{1,0:T(8,128)}) %reduce-scatter.5.cloned.1.call-update) | async-done | bytes 524304 | tf_op jit(solution)/shard_map/reduce_scatter | solution.py:63
  (3 shorter events, 0.0 us)
Async XLA Ops:
  8.0 32.4 %copy-start = (bf16[1024,1024]{1,0:T(8,128)(2,1)S(1)}, bf16[1024,1024]{1,0:T(8,128)(2,1)}, u32[]{:S(2)}) copy-start(bf16[1024,1024]{1,0:T(8,128)(2,1)} %param.7) | copy-start | bytes 6291460
  8.0 25.0 %all-gather.4.cloned.1.call-start = ((), (), s32[]{:S(2)}) async-start(), calls=%async_computation.3 | async-start | bytes 12582912 | tf_op jit(solution)/shard_map/all_gather | solution.py:25
  8.7 62.9 %reduce-scatter.3.cloned.1.call-start = ((), (), s32[]{:S(2)}) async-start(), calls=%async_computation.4 | async-start | bytes 1310720 | tf_op jit(solution)/shard_map/reduce_scatter | solution.py:29
  39.3 1.1 copy-start.2
  40.4 1.9 copy-start.4
  40.4 2.9 copy-start.5
  42.2 67.3 %all-gather.6.cloned.1.call-start = ((), (), s32[]{:S(2)}) async-start(), calls=%async_computation.5 | async-start | bytes 4325376 | tf_op jit(solution)/shard_map/all_gather | solution.py:23
  43.2 230.5 %all-gather.8.cloned.1.call-start = ((), (), s32[]{:S(2)}) async-start(), calls=%async_computation.6 | async-start | bytes 4718592 | tf_op jit(solution)/shard_map/all_gather | solution.py:59
  72.7 80.0 %copy-start.1 = (f32[64,1024]{1,0:T(8,128)S(1)}, f32[64,1024]{1,0:T(8,128)}, u32[]{:S(2)}) copy-start(f32[64,1024]{1,0:T(8,128)} %reduce-scatter.3.cloned.1.call-done) | copy-start | bytes 786436
  152.7 15.0 %copy-start.3 = (f32[256,1024]{1,0:T(8,128)S(1)}, f32[256,1024]{1,0:T(8,128)}, u32[]{:S(2)}) copy-start(f32[256,1024]{1,0:T(8,128)} %copy-done.2) | copy-start | bytes 3145732
  169.8 133.0 %reduce-scatter.5.cloned.1.call-start = ((), (), s32[]{:S(2)}) async-start(), calls=%async_computation.7 | async-start | bytes 4718592 | tf_op jit(solution)/shard_map/reduce_scatter | solution.py:63
  178.1 4.5 %copy-start.6 = (u32[32]{0:T(128)S(1)}, u32[32]{0:T(128)}, u32[]{:S(2)}) copy-start(u32[32]{0:T(128)} %constant.49) | copy-start | bytes 388
  178.1 80.4 %all-to-all-start = ((bf16[256,8,512]{0,2,1:T(8,128)(2,1)}), bf16[256,8,512]{0,2,1:T(8,128)(2,1)}, u32[]{:S(2)}, u32[]{:S(2)}) async-start(bf16[256,8,512]{0,2,1:T(8,128)(2,1)} %bitcast.16), calls=%async_computation.1 | async-start | bytes 4194304 | tf_op jit(solution)/shard_map/all_to_all | solution.py:18
Sparse Core Ops, SparseCore 0:
  10.4 22.5 all-gather.3
  42.4 29.2 reduce-scatter.2
Sparse Core Ops, SparseCore 1:
  46.2 63.3 all-gather.5
  169.9 81.1 all-gather.7
  253.9 48.9 reduce-scatter.4

commit v2 on v1

--- a/solution.py
+++ b/solution.py
@@ -1,6 +1,10 @@
+import functools
+
 import jax
 import jax.numpy as jnp
 from jax import lax
+from jax.experimental import pallas as pl
+from jax.experimental.pallas import tpu as pltpu
 from jax.sharding import PartitionSpec as P
 
 SCALE = 50.0
@@ -11,7 +15,7 @@
     return jax.vjp(jax.nn.gelu, pre)[1](grad)[0]
 
 
-def on_device(features, w_in, w_out, captions, positive):
+def plain(features, w_in, w_out, captions, positive):
     group = ("dp", "row")
     every = ("dp", "row", "col")
     f32 = jnp.float32
@@ -67,6 +71,463 @@
     return (fig_terms, cap_terms, grad_w_in, grad_w_out)
 
 
+MESH = pl.DeviceIdType.MESH
+ROOT = 0.7978845608028654
+CUBE = 0.044715
+TILE = 256
+
+
+def gelu_and_slope(x):
+    t = jnp.tanh(ROOT * (x + CUBE * x * x * x))
+    half = 0.5 * (1.0 + t)
+    return x * half, half + 0.5 * x * (1.0 - t * t) * (ROOT * (1.0 + 3.0 * CUBE * x * x))
+
+
+def remote(src, dst, send, recv, where):
+    return pltpu.make_async_remote_copy(
+        src_ref=src, dst_ref=dst, send_sem=send, recv_sem=recv, device_id=where, device_id_type=MESH
+    )
+
+
+def dot(a, b, ca, cb):
+    return lax.dot_general(a, b, (((ca,), (cb,)), ((), ())), preferred_element_type=jnp.float32)
+
+
+def kernel(nd, nr, nc, feat, w_in, w_out, caps, pos, ids,
+           fig_out, cap_out, gwi, gwo,
+           fsib, psend, precv, pre, slope, hidden, part, esend, erecv, fhat, chat, expo, dlog,
+           dfh, demb, dpre, slices, stage, stat, head, hsum, hsib, hup, hdn,
+           s_f, r_f, s_p, r_p, s_c1, r_c1, s_c2, r_c2, s_c3, r_c3, s_e, r_e,
+           s_x1, r_x1, s_x2, r_x2, s_x3, r_x3, s_d, r_d, s_t, r_t,
+           s_a, r_a, s_b, r_b, s_g, r_g, s_up, r_up, s_dn, r_dn, s_sib, r_sib,
+           s_h, r_h, s_hu, r_hu, s_hd, r_hd):
+    f32, bf16 = jnp.float32, jnp.bfloat16
+    d, r, c = lax.axis_index("dp"), lax.axis_index("row"), lax.axis_index("col")
+    other = 1 - r
+    sib = (d, other, c)
+    rows = feat.shape[0]
+    half = w_in.shape[0]
+    hid = w_in.shape[1]
+    emb = w_out.shape[1]
+    mine = rows // nc
+    cap = caps.shape[0]
+    total = chat.shape[0]
+    width = gwi.shape[0]
+    lanes = gwo.shape[1]
+    tiles = hid // TILE
+
+    def col_of(j):
+        return lax.rem(c + j, nc)
+
+    def dp_of(j):
+        return lax.rem(d + j, nd)
+
+    def at(index, size):
+        return pl.ds(pl.multiple_of(index * size, size), size)
+
+    barrier = pltpu.get_barrier_semaphore()
+    pl.semaphore_signal(barrier, inc=1, device_id=sib, device_id_type=MESH)
+    for j in range(1, nc):
+        pl.semaphore_signal(barrier, inc=1, device_id=(d, r, col_of(j)), device_id_type=MESH)
+    for j in range(1, nd):
+        pl.semaphore_signal(barrier, inc=1, device_id=(dp_of(j), r, c), device_id_type=MESH)
+    pl.semaphore_wait(barrier, nc + nd - 1)
+    sent = []
+
+    def go(*a):
+        cp = remote(*a)
+        cp.start()
+        sent.append(cp)
+        return cp
+
+    cf = go(feat.at[:, at(other, half)], fsib, s_f, r_f, sib)
+    cap32 = caps[...].astype(f32)
+    slot = (r * nc + c) * nd + d
+    chat[at(slot, cap), :] = (
+        cap32 * lax.rsqrt(jnp.sum(cap32 * cap32, axis=1, keepdims=True) + EPS)
+    ).astype(bf16)
+    c1 = [
+        go(chat.at[at(slot, cap)], chat.at[at(slot, cap)], s_c1.at[j], r_c1.at[j], (dp_of(j), r, c))
+        for j in range(1, nd)
+    ]
+    mark = at(d * nr + r, rows)
+    ca, cb = [], []
+    for j in range(1, nd):
+        to = dp_of(j)
+        ca.append(go(feat.at[:, at(to * nr + r, width)], slices.at[mark], s_a.at[j], r_a.at[j], (to, r, c)))
+        cb.append(go(feat.at[:, at(to * nr + other, width)], stage.at[d], s_b.at[j], r_b.at[j], (to, r, c)))
+    go(feat.at[:, at(d * nr + other, width)], slices.at[mark], s_g.at[0], r_g.at[0], sib)
+    slices[mark, :] = feat[:, at(d * nr + r, width)]
+
+    @pl.loop(0, tiles)
+    def _(k):
+        pre[:, at(k, TILE)] = dot(feat[:, at(r, half)], w_in[:, at(k, TILE)], 1, 0)
+
+    cf.wait_recv()
+
+    @pl.loop(0, tiles)
+    def _(k):
+        psend[k] = dot(fsib[...], w_in[:, at(k, TILE)], 1, 0)
+        remote(psend.at[k], precv.at[k], s_p.at[k], r_p.at[k], sib).start()
+
+    @pl.loop(0, tiles)
+    def _(k):
+        remote(psend.at[k], precv.at[k], s_p.at[k], r_p.at[k], sib).wait()
+        x = pre[:, at(k, TILE)] + precv[k]
+        h, g = gelu_and_slope(x)
+        hidden[:, at(k, TILE)] = h.astype(bf16)
+        slope[:, at(k, TILE)] = g
+
+    for cp in c1:
+        cp.wait_recv()
+    c2 = []
+    line = at(r * nc + c, nd * cap)
+    for j in range(1, nc):
+        c2.append(go(chat.at[line], chat.at[line], s_c2.at[j], r_c2.at[j], (d, r, col_of(j))))
+
+    @pl.loop(0, emb // TILE)
+    def _(k):
+        part[:, at(k, TILE)] = dot(hidden[...], w_out[:, at(k, TILE)], 1, 0)
+
+    ce = []
+    for j in range(1, nc):
+        esend[j] = part[at(col_of(j), mine), :].astype(bf16)
+        ce.append(go(esend.at[j], erecv.at[j], s_e.at[j], r_e.at[j], (d, r, col_of(j))))
+    e = part[at(c, mine), :]
+    for j in range(1, nc):
+        ce[j - 1].wait_recv()
+        e = e + erecv[j].astype(f32)
+    inv = lax.rsqrt(jnp.sum(e * e, axis=1, keepdims=True) + EPS)
+    fhat[...] = e * inv
+    for cp in c2:
+        cp.wait_recv()
+    c3 = go(chat.at[at(r, total // nr)], chat.at[at(r, total // nr)], s_c3, r_c3, sib)
+    per = total // nr // TILE
+    fb = fhat[...].astype(bf16)
+
+    def scores(base):
+        @pl.loop(0, per)
+        def _(k):
+            where = at(base * per + k, TILE)
+            expo[:, where] = SCALE * dot(fb, chat[where, :], 1, 1)
+
+    scores(r)
+    c3.wait_recv()
+    scores(other)
+    logits = expo[...]
+    mask = (pos[...] == ids[...]).astype(f32)
+    ex = jnp.exp(logits)
+    picked = mask * logits
+    expo[...] = ex
+    rowsum = jnp.sum(ex, axis=1, keepdims=True)
+    rowpos = jnp.sum(picked, axis=1, keepdims=True)
+    stat[0, 0:1, :] = jnp.sum(ex, axis=0, keepdims=True)
+    stat[0, 1:2, :] = jnp.sum(picked, axis=0, keepdims=True)
+    x1 = go(stat.at[0], stat.at[1], s_x1, r_x1, sib)
+    fig_out[at(c, mine), :] = jnp.broadcast_to(jnp.log(rowsum) - rowpos, (mine, 128))
+    ct = [
+        go(fig_out.at[at(c, mine)], fig_out.at[at(c, mine)], s_t.at[j], r_t.at[j], (d, r, col_of(j)))
+        for j in range(1, nc)
+    ]
+    x1.wait_recv()
+    stat[2] = stat[0] + stat[1]
+    x2 = [
+        go(stat.at[2], stat.at[3 + j], s_x2.at[j], r_x2.at[j], (d, r, col_of(j))) for j in range(1, nc)
+    ]
+    acc = stat[2]
+    for j in range(1, nc):
+        x2[j - 1].wait_recv()
+        acc = acc + stat[3 + j]
+    stat[3] = acc
+    x3 = [
+        go(stat.at[3], stat.at[3 + nc + j], s_x3.at[j], r_x3.at[j], (dp_of(j), r, c))
+        for j in range(1, nd)
+    ]
+    for j in range(1, nd):
+        x3[j - 1].wait_recv()
+        acc = acc + stat[3 + nc + j]
+    colsum = acc[0:1, :]
+    cap_out[...] = jnp.log(colsum) - acc[1:2, :]
+    ex = expo[...]
+    dlog[...] = (ex / rowsum + ex / colsum - 2.0 * mask).astype(bf16)
+
+    @pl.loop(0, emb // TILE)
+    def _(k):
+        dfh[:, at(k, TILE)] = SCALE * dot(dlog[...], chat[:, at(k, TILE)], 1, 0)
+
+    fh = fhat[...]
+    df = dfh[...]
+    demb[at(c, mine), :] = (
+        (df - fh * jnp.sum(fh * df, axis=1, keepdims=True)) * inv
+    ).astype(bf16)
+    cd = [
+        go(demb.at[at(c, mine)], demb.at[at(c, mine)], s_d.at[j], r_d.at[j], (d, r, col_of(j)))
+        for j in range(1, nc)
+    ]
+    for cp in cd:
+        cp.wait_recv()
+
+    def place(k, src, core):
+        return dpre.at[k, at(src * nr + core, rows)]
+
+    def upward(k, s):
+        spot = place(k, d + 1 - s, r)
+        return remote(spot, spot, s_up.at[s, k], r_up.at[s, k], (jnp.minimum(d + 1, nd - 1), r, c))
+
+    def downward(k, s):
+        spot = place(k, d - 1 + s, r)
+        return remote(spot, spot, s_dn.at[s, k], r_dn.at[s, k], (jnp.maximum(d - 1, 0), r, c))
+
+    def across(k, src, n):
+        spot = place(k, src, r)
+        return remote(spot, spot, s_sib.at[n, k], r_sib.at[n, k], sib)
+
+    @pl.loop(0, tiles)
+    def _(k):
+        dh = dot(demb[...], w_out[at(k, TILE), :], 1, 1)
+        dpre[k, at(d * nr + r, rows), :] = (dh * slope[:, at(k, TILE)]).astype(bf16)
+
+        @pl.when(d + 1 < nd)
+        def _():
+            upward(k, 1).start()
+
+        @pl.when(d > 0)
+        def _():
+            downward(k, 1).start()
+
+        across(k, d, 0).start()
+
+    for t in range(nd):
+        both = dot(hidden[...], demb[:, t * nr * lanes : (t + 1) * nr * lanes], 0, 0)
+        low, high = both[:, :lanes], both[:, lanes:]
+        first = r == 0
+        hsum[t] = jnp.where(first, low, high)
+        head[t] = jnp.where(first, high, low).astype(bf16)
+    ch = remote(head, hsib, s_h, r_h, sib)
+    ch.start()
+
+    cg = []
+    for j in range(1, nd):
+        source = lax.rem(d + nd - j, nd)
+        ca[j - 1].wait_recv()
+        cb[j - 1].wait_recv()
+        cg.append(go(stage.at[source], slices.at[at(source * nr + r, rows)], s_g.at[j], r_g.at[j], sib))
+    remote(stage.at[0], stage.at[0], s_g.at[0], r_g.at[0], sib).wait_recv()
+    for cp in cg:
+        cp.wait_recv()
+
+    def product(src, fresh):
+        @pl.loop(0, tiles)
+        def _(k):
+            both = at(src, nr * rows)
+            value = dot(slices[both, :], dpre[k, both, :], 0, 0)
+            if fresh:
+                gwi[:, at(k, TILE)] = value
+            else:
+                gwi[:, at(k, TILE)] += value
+
+    def from_sibling(n):
+        @pl.loop(0, tiles)
+        def _(k):
+            across(k, d, n).wait_recv()
+
+    ch.wait_recv()
+    for t in range(nd):
+        hsum[t] = hsum[t] + hsib[t].astype(f32)
+
+    def hop(t, buf, send, recv, nxt):
+        return remote(head.at[t], buf.at[t], send.at[t], recv.at[t], (nxt, r, c))
+
+    def up_hop(t):
+        return hop(t, hup, s_hu, r_hu, jnp.minimum(d + 1, nd - 1))
+
+    def dn_hop(t):
+        return hop(t, hdn, s_hd, r_hd, jnp.maximum(d - 1, 0))
+
+    ch.wait_send()
+
+    def send_heads():
+        for t in reversed(range(nd)):
+            @pl.when(d < t)
+            def _():
+                @pl.when(d == 0)
+                def _():
+                    head[t] = hsum[t].astype(bf16)
+
+                @pl.when(d > 0)
+                def _():
+                    up_hop(t).wait_recv()
+                    head[t] = (hsum[t] + hup[t].astype(f32)).astype(bf16)
+
+                up_hop(t).start()
+
+        for t in range(nd):
+            @pl.when(d > t)
+            def _():
+                @pl.when(d == nd - 1)
+                def _():
+                    head[t] = hsum[t].astype(bf16)
+
+                @pl.when(d < nd - 1)
+                def _():
+                    dn_hop(t).wait_recv()
+                    head[t] = (hsum[t] + hdn[t].astype(f32)).astype(bf16)
+
+                dn_hop(t).start()
+
+    def relay(s):
+        @pl.loop(0, tiles)
+        def _(k):
+            @pl.when(d - s >= 0)
+            def _():
+                upward(k, s).wait_recv()
+
+                @pl.when(d + 1 < nd)
+                def _():
+                    upward(k, s + 1).start()
+
+                across(k, d - s, 2 * s - 1).start()
+
+            @pl.when(d + s < nd)
+            def _():
+                downward(k, s).wait_recv()
+
+                @pl.when(d > 0)
+                def _():
+                    downward(k, s + 1).start()
+
+                across(k, d + s, 2 * s).start()
+
+    def products(s):
+        @pl.when(d - s >= 0)
+        def _():
+            from_sibling(2 * s - 1)
+            product(d - s, False)
+
+        @pl.when(d + s < nd)
+        def _():
+            from_sibling(2 * s)
+            product(d + s, False)
+
+    from_sibling(0)
+    product(d, True)
+    for s in range(1, nd):
+        relay(s)
+        if s == 1:
+            send_heads()
+        products(s)
+
+    gwo[...] = hsum[d]
+
+    @pl.when(d > 0)
+    def _():
+        up_hop(d).wait_recv()
+        gwo[...] += hup[d].astype(f32)
+
+    @pl.when(d < nd - 1)
+    def _():
+        dn_hop(d).wait_recv()
+        gwo[...] += hdn[d].astype(f32)
+
+    for cp in ct:
+        cp.wait_recv()
+    for cp in sent:
+        cp.wait_send()
+    for t in range(nd):
+        @pl.when(d < t)
+        def _():
+            up_hop(t).wait_send()
+
+        @pl.when(d > t)
+        def _():
+            dn_hop(t).wait_send()
+
+    @pl.loop(0, tiles)
+    def _(k):
+        across(k, d, 0).wait_send()
+        for s in range(1, nd + 1):
+            if s < nd:
+                @pl.when(d - s >= 0)
+                def _():
+                    across(k, d - s, 2 * s - 1).wait_send()
+
+                @pl.when(d + s < nd)
+                def _():
+                    across(k, d + s, 2 * s).wait_send()
+
+            @pl.when((d + 1 < nd) & (d + 1 - s >= 0))
+            def _():
+                upward(k, s).wait_send()
+
+            @pl.when((d > 0) & (d - 1 + s < nd))
+            def _():
+                downward(k, s).wait_send()
+
+
+def joined(features, w_in, w_out, captions, positive):
+    nd, nr, nc = (lax.axis_size(a) for a in ("dp", "row", "col"))
+    d, r, c = (lax.axis_index(a) for a in ("dp", "row", "col"))
+    rows, din = features.shape
+    half, hid = w_in.shape
+    emb = w_out.shape[1]
+    cap = captions.shape[0]
+    mine = rows // nc
+    total = nd * nr * nc * cap
+    width, lanes = din // (nd * nr), emb // (nd * nr)
+    tiles = hid // TILE
+    pos = lax.dynamic_slice_in_dim(positive, c * mine, mine, 0)[:, None]
+    ids = jnp.arange(total, dtype=jnp.int32).reshape(nd, nr, nc, cap)
+    ids = ids.transpose(1, 2, 0, 3).reshape(1, total)
+    f32, bf16 = jnp.float32, jnp.bfloat16
+    V, D = pltpu.VMEM, pltpu.SemaphoreType.DMA
+    one = D(())
+    scratch = [
+        V((rows, half), bf16), V((tiles, rows, TILE), f32), V((tiles, rows, TILE), f32),
+        V((rows, hid), f32), V((rows, hid), f32), V((rows, hid), bf16), V((rows, emb), f32),
+        V((nc, mine, emb), bf16), V((nc, mine, emb), bf16), V((mine, emb), f32),
+        V((total, emb), bf16), V((mine, total), f32), V((mine, total), bf16),
+        V((mine, emb), f32), V((rows, emb), bf16), V((tiles, nd * nr * rows, TILE), bf16),
+        V((nd * nr * rows, width), bf16), V((nd, rows, width), bf16),
+        V((3 + nc + nd, 2, total), f32),
+        V((nd, hid, lanes), bf16), V((nd, hid, lanes), f32), V((nd, hid, lanes), bf16),
+        V((nd, hid, lanes), bf16), V((nd, hid, lanes), bf16),
+    ]
+    sems = [
+        one, D((tiles,)), D((nd,)), D((nc,)), one, D((nc,)),
+        one, D((nc,)), D((nd,)), D((nc,)), D((nc,)),
+        D((nd,)), D((nd,)), D((nd,)), D((nd + 1, tiles)), D((nd + 1, tiles)), D((2 * nd, tiles)),
+        one, D((nd,)), D((nd,)),
+    ]
+    scratch += [s for s in sems for _ in range(2)]
+    fig, capt, gwi, gwo = pl.pallas_call(
+        functools.partial(kernel, nd, nr, nc),
+        out_shape=(
+            jax.ShapeDtypeStruct((rows, 128), f32),
+            jax.ShapeDtypeStruct((1, total), f32),
+            jax.ShapeDtypeStruct((width, hid), f32),
+            jax.ShapeDtypeStruct((hid, lanes), f32),
+        ),
+        in_specs=[pl.BlockSpec(memory_space=V)] * 6,
+        out_specs=[pl.BlockSpec(memory_space=V)] * 4,
+        scratch_shapes=scratch,
+        compiler_params=pltpu.CompilerParams(
+            collective_id=0, has_side_effects=True, vmem_limit_bytes=60 * 2**20
+        ),
+    )(features, w_in, w_out, captions, pos, ids)
+    slot = (r * nc + c) * nd + d
+    cap_terms = lax.dynamic_slice_in_dim(capt[0], slot * cap, cap, 0)
+    return fig[:, 0], cap_terms, gwi, gwo
+
+
+def on_device(features, w_in, w_out, captions, positive):
+    nd, nr, nc = (lax.axis_size(a) for a in ("dp", "row", "col"))
+    groups = nd * nr
+    small = groups * features.shape[0] <= 2048 and nr == 2 and nd > 1 and nc > 1
+    even = features.shape[1] % (128 * groups) == 0 and w_out.shape[1] % (128 * groups) == 0
+    body = joined if small and even else plain
+    return body(features, w_in, w_out, captions, positive)
+
+
 def solution(mesh):
     placed = (
         P(("dp", "row"), None),

time: 311 us -> 159 us (0.51)
  waiting for transfers between devices: 184 us -> 0 us
  Pallas kernels: 0 us -> 149 us
  blocking collectives: 61.4 us -> 0 us
  matrix products: 28.1 us -> 0 us
  between operations: 16.4 us -> 0.66 us
  starting transfers between devices: 4.7 us -> 0 us
  local copies, waits for them, and re-layouts: 12.8 us -> 8.92 us
    pallas_call x0 -> x1, Pallas kernels: none -> 149 us  [joined(): pl.pallas_call(functools.partial(kernel, nd, nr, nc), out_shape=(jax.Shap...]
    all_to_all x1 -> x0, waiting for transfers between devices: 74.7 us -> none  [on_device(): slices = lax.all_to_all(features, group, 1, 0, tiled=True)]
    all_gather x3 -> x0, waiting for transfers between devices: 61 us -> none  [the longest x1 36.8 us: on_device(): chat = lax.all_gather(chat_local, every, axis=0, tiled=True)]
    reduce_scatter x2 -> x0, waiting for transfers between devices: 47.8 us -> none  [the longest x1 28.3 us: on_device(): emb = lax.psum_scatter(part, 'col', scatter_dimension=0, tiled=True)]
    psum x1 -> x0, blocking collectives: 39.3 us -> none  [on_device(): lax.psum((jnp.sum(expo, axis=0), jnp.sum(picked, axis=0)), every)]
    dot_general x7 -> x0, matrix products: 28.1 us -> none  [the longest x1 6.69 us: on_device(): lax.dot_general(slices, dpre_all, (((0,), (0,)), ((), ())), preferred_ele...]
    all_gather x1 -> x0, blocking collectives: 11.6 us -> none  [on_device(): demb = lax.all_gather(demb, 'col', axis=0, tiled=True)]
    unnamed x1 -> x0, blocking collectives: 10.5 us -> none
  transfers between devices with their start and end apart: 6 -> 0, of which waited for: 5 -> 0; matrix products, arithmetic and copies ran while one was open for 8% -> 0% of each run, Pallas kernels for 0% -> 0%
where the time goes in v2:
time: 159 us; the launch traced here: 158 us
  Pallas kernels  149 us (94%)
  local copies, waits for them, and re-layouts  8.92 us (6%)
    pallas_call x1, Pallas kernels, joined(): pl.pallas_call(functools.partial(kernel, nd, nr, nc), out_shape=(jax.Shap...  149 us
    unnamed x6, local copies, waits for them, and re-layouts  4.68 us

profile of v2, /device:TPU:0, one launch (start us, length us, event | category | flops | bytes accessed | tf_op | source)
XLA Modules:
  0.0 158.4 jit_solution(1939955794396230147)
XLA Ops:
  0.6 0.0 copy-start
  0.7 0.7 copy-done
  1.3 0.1 dynamic-slice_bitcast_fusion.1
  1.4 0.7 reshape.103.ids
  2.1 0.7 copy.10.pos
  2.8 148.8 %shard_map.84 = (f32[256,128]{1,0:T(8,128)}, f32[1,2048]{1,0:T(1,128)}, f32[512,1024]{1,0:T(8,128)}, f32[1024,128]{1,0:T(8,128)}) custom-call(bf16[256,4096]{1,0:T(8,128)(2,1)} %feat.1, bf16[2048,1024]{1,0:T(8,128)(2,1)} %w_in.1, bf16[1024,1024]{1,0:T(8,128)(2,1)} %w_out.1, bf16[64,1024]{1,0:T(8,128)(2,1)} %caps.1, s32[64,1]{1,0:T(8,128)} %copy.10.pos, ...), custom_call_target="tpu_custom_call" | custom-call | tf_op jit(solution)/shard_map/pallas_call | solution.py:502
  151.6 1.6 slice_reduce_fusion
  153.2 1.2 dynamic-slice_bitcast_fusion
  154.4 0.0 copy-start.1
  154.4 3.2 %copy.13 = f32[512,1024]{1,0:T(8,128)} copy(f32[512,1024]{1,0:T(8,128)} %get-tuple-element.18) | data formatting | bytes 4194304
  157.6 0.0 copy-done.1
  157.6 0.8 copy.14
  (1 shorter events, 0.0 us)
Async XLA Ops:
  0.6 0.7 copy-start
  154.4 3.2 %copy-start.1 = (f32[1024,128]{1,0:T(8,128)S(1)}, f32[1024,128]{1,0:T(8,128)}, u32[]{:S(2)}) copy-start(f32[1024,128]{1,0:T(8,128)} %get-tuple-element.19) | copy-start | bytes 1572868

commit v3 on v2

--- a/solution.py
+++ b/solution.py
@@ -99,7 +99,7 @@
            dfh, demb, dpre, slices, stage, stat, head, hsum, hsib, hup, hdn,
            s_f, r_f, s_p, r_p, s_c1, r_c1, s_c2, r_c2, s_c3, r_c3, s_e, r_e,
            s_x1, r_x1, s_x2, r_x2, s_x3, r_x3, s_d, r_d, s_t, r_t,
-           s_a, r_a, s_b, r_b, s_g, r_g, s_up, r_up, s_dn, r_dn, s_sib, r_sib,
+           s_a, r_a, s_b, r_b, s_g, r_g, s_q, r_q, s_up, r_up, s_dn, r_dn, s_sib, r_sib,
            s_h, r_h, s_hu, r_hu, s_hd, r_hd):
     f32, bf16 = jnp.float32, jnp.bfloat16
     d, r, c = lax.axis_index("dp"), lax.axis_index("row"), lax.axis_index("col")
@@ -150,40 +150,53 @@
         go(chat.at[at(slot, cap)], chat.at[at(slot, cap)], s_c1.at[j], r_c1.at[j], (dp_of(j), r, c))
         for j in range(1, nd)
     ]
+    c2 = [[
+        go(chat.at[at(slot, cap)], chat.at[at(slot, cap)], s_c2.at[j, 0], r_c2.at[j, 0], (d, r, col_of(j)))
+        for j in range(1, nc)
+    ]]
     mark = at(d * nr + r, rows)
+    slices[mark, :] = feat[:, at(d * nr + r, width)]
+
+    @pl.loop(0, tiles)
+    def _(k):
+        pre[:, at(k, TILE)] = dot(feat[:, at(r, half)], w_in[:, at(k, TILE)], 1, 0)
+
+    cf.wait_recv()
+
+    @pl.loop(0, tiles)
+    def _(k):
+        psend[k] = dot(fsib[...], w_in[:, at(k, TILE)], 1, 0)
+        remote(psend.at[k], precv.at[k], s_p.at[k], r_p.at[k], sib).start()
+
+    @pl.loop(0, tiles)
+    def _(k):
+        remote(psend.at[k], precv.at[k], s_p.at[k], r_p.at[k], sib).wait()
+        x = pre[:, at(k, TILE)] + precv[k]
+        pre[:, at(k, TILE)] = x
+        hidden[:, at(k, TILE)] = gelu_and_slope(x)[0].astype(bf16)
+
+    for i in range(1, nd):
+        c1[i - 1].wait_recv()
+        got = at((r * nc + c) * nd + lax.rem(d + nd - i, nd), cap)
+        c2.append([
+            go(chat.at[got], chat.at[got], s_c2.at[j, i], r_c2.at[j, i], (d, r, col_of(j)))
+            for j in range(1, nc)
+        ])
+
+    def line(core, j):
+        return at(core * nc + lax.rem(c + nc - j, nc), nd * cap)
+
+    own = line(r, 0)
+    c3 = [go(chat.at[own], chat.at[own], s_c3.at[0], r_c3.at[0], sib)]
+    quarter = at(c, mine)
     ca, cb = [], []
     for j in range(1, nd):
         to = dp_of(j)
-        ca.append(go(feat.at[:, at(to * nr + r, width)], slices.at[mark], s_a.at[j], r_a.at[j], (to, r, c)))
-        cb.append(go(feat.at[:, at(to * nr + other, width)], stage.at[d], s_b.at[j], r_b.at[j], (to, r, c)))
+        ca.append(go(feat.at[quarter, at(to * nr + r, width)],
+                     slices.at[at((d * nr + r) * nc + c, mine)], s_a.at[j], r_a.at[j], (to, r, c)))
+        cb.append(go(feat.at[quarter, at(to * nr + other, width)],
+                     stage.at[d], s_b.at[j], r_b.at[j], (to, r, c)))
     go(feat.at[:, at(d * nr + other, width)], slices.at[mark], s_g.at[0], r_g.at[0], sib)
-    slices[mark, :] = feat[:, at(d * nr + r, width)]
-
-    @pl.loop(0, tiles)
-    def _(k):
-        pre[:, at(k, TILE)] = dot(feat[:, at(r, half)], w_in[:, at(k, TILE)], 1, 0)
-
-    cf.wait_recv()
-
-    @pl.loop(0, tiles)
-    def _(k):
-        psend[k] = dot(fsib[...], w_in[:, at(k, TILE)], 1, 0)
-        remote(psend.at[k], precv.at[k], s_p.at[k], r_p.at[k], sib).start()
-
-    @pl.loop(0, tiles)
-    def _(k):
-        remote(psend.at[k], precv.at[k], s_p.at[k], r_p.at[k], sib).wait()
-        x = pre[:, at(k, TILE)] + precv[k]
-        h, g = gelu_and_slope(x)
-        hidden[:, at(k, TILE)] = h.astype(bf16)
-        slope[:, at(k, TILE)] = g
-
-    for cp in c1:
-        cp.wait_recv()
-    c2 = []
-    line = at(r * nc + c, nd * cap)
-    for j in range(1, nc):
-        c2.append(go(chat.at[line], chat.at[line], s_c2.at[j], r_c2.at[j], (d, r, col_of(j))))
 
     @pl.loop(0, emb // TILE)
     def _(k):
@@ -193,27 +206,31 @@
     for j in range(1, nc):
         esend[j] = part[at(col_of(j), mine), :].astype(bf16)
         ce.append(go(esend.at[j], erecv.at[j], s_e.at[j], r_e.at[j], (d, r, col_of(j))))
+
+    @pl.loop(0, tiles)
+    def _(k):
+        slope[:, at(k, TILE)] = gelu_and_slope(pre[:, at(k, TILE)])[1]
+
     e = part[at(c, mine), :]
     for j in range(1, nc):
         ce[j - 1].wait_recv()
         e = e + erecv[j].astype(f32)
     inv = lax.rsqrt(jnp.sum(e * e, axis=1, keepdims=True) + EPS)
     fhat[...] = e * inv
-    for cp in c2:
-        cp.wait_recv()
-    c3 = go(chat.at[at(r, total // nr)], chat.at[at(r, total // nr)], s_c3, r_c3, sib)
-    per = total // nr // TILE
     fb = fhat[...].astype(bf16)
 
-    def scores(base):
-        @pl.loop(0, per)
-        def _(k):
-            where = at(base * per + k, TILE)
-            expo[:, where] = SCALE * dot(fb, chat[where, :], 1, 1)
-
-    scores(r)
-    c3.wait_recv()
-    scores(other)
+    def scores(where):
+        expo[:, where] = SCALE * dot(fb, chat[where, :], 1, 1)
+
+    scores(own)
+    for j in range(1, nc):
+        for i in range(nd):
+            c2[i][j - 1].wait_recv()
+        c3.append(go(chat.at[line(r, j)], chat.at[line(r, j)], s_c3.at[j], r_c3.at[j], sib))
+        scores(line(r, j))
+    for j in range(nc):
+        c3[j].wait_recv()
+        scores(line(other, j))
     logits = expo[...]
     mask = (pos[...] == ids[...]).astype(f32)
     ex = jnp.exp(logits)
@@ -306,15 +323,25 @@
     ch = remote(head, hsib, s_h, r_h, sib)
     ch.start()
 
-    cg = []
+    def share(source, core, n):
+        spot = at((source * nr + core) * nc + c, mine)
+        return [
+            go(slices.at[spot], slices.at[spot], s_q.at[q, n], r_q.at[q, n], (d, r, col_of(q)))
+            for q in range(1, nc)
+        ]
+
+    cg, cq = [], []
     for j in range(1, nd):
         source = lax.rem(d + nd - j, nd)
         ca[j - 1].wait_recv()
         cb[j - 1].wait_recv()
-        cg.append(go(stage.at[source], slices.at[at(source * nr + r, rows)], s_g.at[j], r_g.at[j], sib))
-    remote(stage.at[0], stage.at[0], s_g.at[0], r_g.at[0], sib).wait_recv()
-    for cp in cg:
-        cp.wait_recv()
+        spot = at((source * nr + r) * nc + c, mine)
+        cg.append(go(stage.at[source], slices.at[spot], s_g.at[j], r_g.at[j], sib))
+        cq += share(source, r, j)
+    for j in range(1, nd):
+        cg[j - 1].wait_recv()
+        cq += share(lax.rem(d + nd - j, nd), other, nd + j)
+    remote(slices.at[mark], slices.at[mark], s_g.at[0], r_g.at[0], sib).wait_recv()
 
     def product(src, fresh):
         @pl.loop(0, tiles)
@@ -415,6 +442,8 @@
         relay(s)
         if s == 1:
             send_heads()
+            for cp in cq:
+                cp.wait_recv()
         products(s)
 
     gwo[...] = hsum[d]
@@ -487,15 +516,15 @@
         V((nc, mine, emb), bf16), V((nc, mine, emb), bf16), V((mine, emb), f32),
         V((total, emb), bf16), V((mine, total), f32), V((mine, total), bf16),
         V((mine, emb), f32), V((rows, emb), bf16), V((tiles, nd * nr * rows, TILE), bf16),
-        V((nd * nr * rows, width), bf16), V((nd, rows, width), bf16),
+        V((nd * nr * rows, width), bf16), V((nd, mine, width), bf16),
         V((3 + nc + nd, 2, total), f32),
         V((nd, hid, lanes), bf16), V((nd, hid, lanes), f32), V((nd, hid, lanes), bf16),
         V((nd, hid, lanes), bf16), V((nd, hid, lanes), bf16),
     ]
     sems = [
-        one, D((tiles,)), D((nd,)), D((nc,)), one, D((nc,)),
+        one, D((tiles,)), D((nd,)), D((nc, nd)), D((nc,)), D((nc,)),
         one, D((nc,)), D((nd,)), D((nc,)), D((nc,)),
-        D((nd,)), D((nd,)), D((nd,)), D((nd + 1, tiles)), D((nd + 1, tiles)), D((2 * nd, tiles)),
+        D((nd,)), D((nd,)), D((nd,)), D((nc, 2 * nd)), D((nd + 1, tiles)), D((nd + 1, tiles)), D((2 * nd, tiles)),
         one, D((nd,)), D((nd,)),
     ]
     scratch += [s for s in sems for _ in range(2)]
@@ -523,7 +552,7 @@
     nd, nr, nc = (lax.axis_size(a) for a in ("dp", "row", "col"))
     groups = nd * nr
     small = groups * features.shape[0] <= 2048 and nr == 2 and nd > 1 and nc > 1
-    even = features.shape[1] % (128 * groups) == 0 and w_out.shape[1] % (128 * groups) == 0
+    even = (nd * captions.shape[0]) % 128 == 0 and features.shape[1] % (128 * groups) == 0 and w_out.shape[1] % (128 * groups) == 0
     body = joined if small and even else plain
     return body(features, w_in, w_out, captions, positive)
 

time: 159 us -> 128 us (0.81)
  Pallas kernels: 149 us -> 118 us
    pallas_call x1, Pallas kernels: 149 us -> 118 us  [joined(): pl.pallas_call(functools.partial(kernel, nd, nr, nc), out_shape=(jax.Shap...]
where the time goes in v3:
time: 128 us; the launch traced here: 127 us
  Pallas kernels  118 us (92%)
  local copies, waits for them, and re-layouts  8.92 us (7%)
    pallas_call x1, Pallas kernels, joined(): pl.pallas_call(functools.partial(kernel, nd, nr, nc), out_shape=(jax.Shap...  118 us
    unnamed x6, local copies, waits for them, and re-layouts  4.68 us

profile of v3, /device:TPU:0, one launch (start us, length us, event | category | flops | bytes accessed | tf_op | source)
XLA Modules:
  0.0 127.3 jit_solution(3953964897200034723)
XLA Ops:
  0.6 0.0 copy-start
  0.7 0.7 copy-done
  1.3 0.1 dynamic-slice_bitcast_fusion.1
  1.4 0.7 reshape.103.ids
  2.1 0.7 copy.10.pos
  2.8 117.7 %shard_map.84 = (f32[256,128]{1,0:T(8,128)}, f32[1,2048]{1,0:T(1,128)}, f32[512,1024]{1,0:T(8,128)}, f32[1024,128]{1,0:T(8,128)}) custom-call(bf16[256,4096]{1,0:T(8,128)(2,1)} %feat.1, bf16[2048,1024]{1,0:T(8,128)(2,1)} %w_in.1, bf16[1024,1024]{1,0:T(8,128)(2,1)} %w_out.1, bf16[64,1024]{1,0:T(8,128)(2,1)} %caps.1, s32[64,1]{1,0:T(8,128)} %copy.10.pos, ...), custom_call_target="tpu_custom_call" | custom-call | tf_op jit(solution)/shard_map/pallas_call | solution.py:531
  120.5 1.6 %slice_reduce_fusion = f32[256]{0:T(256)} fusion(f32[256,128]{1,0:T(8,128)} %get-tuple-element.8), kind=kLoop, calls=%fused_computation | loop fusion | bytes 2048 | tf_op jit(solution)/shard_map/slice | solution.py:548
  122.1 1.2 dynamic-slice_bitcast_fusion
  123.3 0.0 copy-start.1
  123.3 3.2 %copy.13 = f32[512,1024]{1,0:T(8,128)} copy(f32[512,1024]{1,0:T(8,128)} %get-tuple-element.18) | data formatting | bytes 4194304
  126.5 0.0 copy-done.1
  126.5 0.8 copy.14
  (1 shorter events, 0.0 us)
Async XLA Ops:
  0.6 0.7 copy-start
  123.3 3.2 %copy-start.1 = (f32[1024,128]{1,0:T(8,128)S(1)}, f32[1024,128]{1,0:T(8,128)}, u32[]{:S(2)}) copy-start(f32[1024,128]{1,0:T(8,128)} %get-tuple-element.19) | copy-start | bytes 1572868

commit v4 on v3

--- a/solution.py
+++ b/solution.py
@@ -373,33 +373,31 @@
 
     ch.wait_send()
 
-    def send_heads():
+    for t in reversed(range(1, nd)):
+        @pl.when(d == 0)
+        def _():
+            head[t] = hsum[t].astype(bf16)
+            up_hop(t).start()
+
+    for t in range(nd - 1):
+        @pl.when(d == nd - 1)
+        def _():
+            head[t] = hsum[t].astype(bf16)
+            dn_hop(t).start()
+
+    def pass_heads():
         for t in reversed(range(nd)):
-            @pl.when(d < t)
+            @pl.when((d > 0) & (d < t))
             def _():
-                @pl.when(d == 0)
-                def _():
-                    head[t] = hsum[t].astype(bf16)
-
-                @pl.when(d > 0)
-                def _():
-                    up_hop(t).wait_recv()
-                    head[t] = (hsum[t] + hup[t].astype(f32)).astype(bf16)
-
+                up_hop(t).wait_recv()
+                head[t] = (hsum[t] + hup[t].astype(f32)).astype(bf16)
                 up_hop(t).start()
 
         for t in range(nd):
-            @pl.when(d > t)
+            @pl.when((d < nd - 1) & (d > t))
             def _():
-                @pl.when(d == nd - 1)
-                def _():
-                    head[t] = hsum[t].astype(bf16)
-
-                @pl.when(d < nd - 1)
-                def _():
-                    dn_hop(t).wait_recv()
-                    head[t] = (hsum[t] + hdn[t].astype(f32)).astype(bf16)
-
+                dn_hop(t).wait_recv()
+                head[t] = (hsum[t] + hdn[t].astype(f32)).astype(bf16)
                 dn_hop(t).start()
 
     def relay(s):
@@ -438,13 +436,15 @@
 
     from_sibling(0)
     product(d, True)
-    for s in range(1, nd):
+    for s in range(1, nd - 1):
         relay(s)
-        if s == 1:
-            send_heads()
-            for cp in cq:
-                cp.wait_recv()
+    pass_heads()
+    for cp in cq:
+        cp.wait_recv()
+    for s in range(1, nd - 1):
         products(s)
+    relay(nd - 1)
+    products(nd - 1)
 
     gwo[...] = hsum[d]
 

time: 128 us -> 118 us (0.922)
  Pallas kernels: 118 us -> 108 us
    pallas_call x1, Pallas kernels: 118 us -> 108 us  [joined(): pl.pallas_call(functools.partial(kernel, nd, nr, nc), out_shape=(jax.Shap...]
where the time goes in v4:
time: 118 us; the launch traced here: 117 us
  Pallas kernels  108 us (92%)
  local copies, waits for them, and re-layouts  8.92 us (8%)
    pallas_call x1, Pallas kernels, joined(): pl.pallas_call(functools.partial(kernel, nd, nr, nc), out_shape=(jax.Shap...  108 us
    unnamed x6, local copies, waits for them, and re-layouts  4.68 us

profile of v4, /device:TPU:0, one launch (start us, length us, event | category | flops | bytes accessed | tf_op | source)
XLA Modules:
  0.0 117.5 jit_solution(13371563565500922286)
XLA Ops:
  0.6 0.0 copy-start
  0.7 0.7 copy-done
  1.3 0.1 dynamic-slice_bitcast_fusion.1
  1.4 0.7 reshape.103.ids
  2.1 0.7 copy.10.pos
  2.8 107.9 %shard_map.84 = (f32[256,128]{1,0:T(8,128)}, f32[1,2048]{1,0:T(1,128)}, f32[512,1024]{1,0:T(8,128)}, f32[1024,128]{1,0:T(8,128)}) custom-call(bf16[256,4096]{1,0:T(8,128)(2,1)} %feat.1, bf16[2048,1024]{1,0:T(8,128)(2,1)} %w_in.1, bf16[1024,1024]{1,0:T(8,128)(2,1)} %w_out.1, bf16[64,1024]{1,0:T(8,128)(2,1)} %caps.1, s32[64,1]{1,0:T(8,128)} %copy.10.pos, ...), custom_call_target="tpu_custom_call" | custom-call | tf_op jit(solution)/shard_map/pallas_call | solution.py:531
  110.7 1.6 %slice_reduce_fusion = f32[256]{0:T(256)} fusion(f32[256,128]{1,0:T(8,128)} %get-tuple-element.8), kind=kLoop, calls=%fused_computation | loop fusion | bytes 2048 | tf_op jit(solution)/shard_map/slice | solution.py:548
  112.3 1.2 %dynamic-slice_bitcast_fusion = f32[64]{0:T(128)} fusion(f32[1,2048]{1,0:T(1,128)} %get-tuple-element.9, s32[]{:T(128)S(6)} %select_n.7), kind=kLoop, calls=%fused_computation.2 | loop fusion | bytes 516 | tf_op jit(solution)/shard_map/dynamic_slice | solution.py:547
  113.5 0.0 copy-start.1
  113.5 3.2 %copy.13 = f32[512,1024]{1,0:T(8,128)} copy(f32[512,1024]{1,0:T(8,128)} %get-tuple-element.18) | data formatting | bytes 4194304
  116.7 0.0 copy-done.1
  116.7 0.8 copy.14
  (1 shorter events, 0.0 us)
Async XLA Ops:
  0.6 0.7 copy-start
  113.5 3.2 %copy-start.1 = (f32[1024,128]{1,0:T(8,128)S(1)}, f32[1024,128]{1,0:T(8,128)}, u32[]{:S(2)}) copy-start(f32[1024,128]{1,0:T(8,128)} %get-tuple-element.19) | copy-start | bytes 1572868
